TPU v7x, 32 devices: a whole 2x2x4 slice. The times are simulated.
32 devices in a mesh: dp: 8 (over y, x, core), fsdp: 4 (over z).
Axes of the slice: x: 2, y: 2, z: 4, core: 2. Of those that a mesh axis runs over, the one named last changes fastest.
Arguments:
- unit_ids: int32 [4, 8, 8, 32], P('fsdp', 'dp'), may hold values from 0 to 2047
- session_ids: int32 [4, 8, 8, 32], P('fsdp', 'dp'), may hold values from 0 to 63
- counts: int32 [4, 8, 8], P('fsdp', 'dp'), may hold values from 8 to 32, as said below
- targets: int32 [4, 8, 256, 512], P('fsdp', 'dp'), may hold values 0 or 1
- unit_table: bfloat16 [2048, 1024], replicated, may hold values from -6 to 6
- session_table: bfloat16 [64, 1024], replicated, may hold values from -4 to 4
- attn_weights: bfloat16 [4, 1024, 1024], P(None, 'fsdp'), may hold values from -0.1875 to 0.1875
- read_weight: bfloat16 [1024, 512], P('fsdp'), may hold values from -0.1875 to 0.1875
- latents: bfloat16 [256, 1024], P('fsdp')
Outputs:
- event_grad: bfloat16 [4, 8, 8, 32, 1024], P('fsdp', 'dp')
- grad_attn: float32 [4, 1024, 1024], P(None, 'fsdp')
- grad_read: float32 [1024, 512], P('fsdp')
- grad_latents: float32 [256, 1024], P('fsdp')
Inputs may be any that keep to these rules, and one draw needn't show every extreme that they name: counts[f, s, d] is how many of the slots from source s to window d are live (the first ones); in every row (f, s) some window receives exactly 32.
All inputs are finite; a program needn't handle non-finite values. No bound on the sum of `targets` on one device may be relied on, other than what follows from the above.
Results may differ from a plain program's by a relative error of at most 0.012.
The roundings to bfloat16 on the way count: a program that leaves them out, or rounds other values in their place, can miss the bound.
Values may be sent and summed in bfloat16 or wider, within the bound.
A program may use at most 192 MiB of HBM per device.

v0:
```python
import jax
import jax.numpy as jnp
from jax import lax
from jax.sharding import PartitionSpec as P

HEADS = 16


eps = 1e-05


def rms_scale(rows):
    return lax.rsqrt(jnp.mean(rows * rows, axis=-1, keepdims=True) + eps)


def rms_back(rows, factor, grad_out):
    cubed = factor * factor * factor
    return factor * grad_out - rows * cubed * jnp.mean(grad_out * rows, axis=-1, keepdims=True)


def matmul(left, right):
    return jnp.dot(left, right, preferred_element_type=jnp.float32)


def contract(form, left, right):
    return jnp.einsum(form, left, right, preferred_element_type=jnp.float32)


def live_mask(got_counts, slot_count):
    return (jnp.arange(slot_count, dtype=jnp.int32)[None, :] < got_counts[:, None]).reshape(-1)


def event_front(tokens, w_key, w_value):
    token_rows = tokens.astype(jnp.float32)
    factor = rms_scale(token_rows)
    normed = (token_rows * factor).astype(jnp.bfloat16)
    key_rows = matmul(normed, w_key).astype(jnp.bfloat16)
    value_rows = matmul(normed, w_value).astype(jnp.bfloat16)
    return (normed, factor, key_rows, value_rows)


def event_back(tokens, factor, normed, grad_keys, grad_values, w_key, w_value):
    grad_wkey = matmul(normed.T, grad_keys)
    grad_wvalue = matmul(normed.T, grad_values)
    grad_normed = matmul(grad_keys, w_key.T) + matmul(grad_values, w_value.T)
    grad_tokens = rms_back(tokens.astype(jnp.float32), factor, grad_normed).astype(jnp.bfloat16)
    return (grad_wkey, grad_wvalue, grad_tokens)


def latent_side(latents, key_rows, value_rows, live_slots, target, w_query, w_out, w_read):
    latent_rows, model_width = latents.shape
    head_dim = model_width // HEADS
    head_factor = head_dim ** (-0.5)
    query = matmul(latents, w_query).astype(jnp.bfloat16)
    query_heads = query.reshape(latent_rows, HEADS, head_dim)
    key_heads = key_rows.reshape(-1, HEADS, head_dim)
    value_heads = value_rows.reshape(-1, HEADS, head_dim)
    scores = contract("qhd,khd->hqk", query_heads, key_heads) * head_factor
    live_wide = live_slots[None, None, :]
    masked = jnp.where(live_wide, scores, -1e30)
    row_max = jnp.max(masked, axis=-1, keepdims=True)
    weights = jnp.where(live_wide, jnp.exp(masked - row_max), 0.0)
    probs = weights / jnp.sum(weights, axis=-1, keepdims=True)
    probs_low = probs.astype(jnp.bfloat16)
    mixed_heads = (
        contract("hqk,khd->qhd", probs_low, value_heads)
        .reshape(latent_rows, model_width)
        .astype(jnp.bfloat16)
    )
    residual = latents.astype(jnp.float32) + matmul(mixed_heads, w_out)
    latent_factor = rms_scale(residual)
    normed = (residual * latent_factor).astype(jnp.bfloat16)
    logits = matmul(normed, w_read)
    grad_logits = (
        (jax.nn.sigmoid(logits) - target.astype(jnp.float32)) * latent_rows ** (-0.5)
    ).astype(jnp.bfloat16)
    grad_wread = matmul(normed.T, grad_logits)
    grad_normed = matmul(grad_logits, w_read.T)
    grad_residual = rms_back(residual, latent_factor, grad_normed)
    grad_res_low = grad_residual.astype(jnp.bfloat16)
    grad_wout = matmul(mixed_heads.T, grad_res_low)
    grad_mixed = (
        matmul(grad_res_low, w_out.T).astype(jnp.bfloat16).reshape(latent_rows, HEADS, head_dim)
    )
    grad_probs = contract("qhd,khd->hqk", grad_mixed, value_heads)
    grad_values = (
        contract("hqk,qhd->khd", probs_low, grad_mixed)
        .reshape(-1, model_width)
        .astype(jnp.bfloat16)
    )
    inner = jnp.sum(grad_probs * probs, axis=-1, keepdims=True)
    grad_scores = (probs * (grad_probs - inner) * head_factor).astype(jnp.bfloat16)
    grad_query = (
        contract("hqk,khd->qhd", grad_scores, key_heads)
        .reshape(latent_rows, model_width)
        .astype(jnp.bfloat16)
    )
    grad_keys = (
        contract("hqk,qhd->khd", grad_scores, query_heads)
        .reshape(-1, model_width)
        .astype(jnp.bfloat16)
    )
    grad_wquery = matmul(latents.T, grad_query)
    grad_latents = grad_residual + matmul(grad_query, w_query.T)
    return (grad_keys, grad_values, grad_wquery, grad_wout, grad_wread, grad_latents)


def on_device(
    unit_ids,
    session_ids,
    counts,
    targets,
    unit_table,
    session_table,
    attn_weights,
    read_weight,
    latents,
):
    group_size = lax.axis_size("dp")
    slot_count = unit_ids.shape[-1]
    model_width = unit_table.shape[1]
    event_total = group_size * slot_count
    unit_rows = unit_ids.reshape(event_total)
    session_rows = session_ids.reshape(event_total)
    session_onehot = (
        session_rows[:, None] == jnp.arange(session_table.shape[0], dtype=jnp.int32)[None, :]
    ).astype(jnp.bfloat16)
    tokens = (
        jnp.take(unit_table, unit_rows, axis=0).astype(jnp.float32)
        + matmul(session_onehot, session_table)
    ).astype(jnp.bfloat16)
    sent_counts = counts.reshape(group_size)
    target = targets.reshape(targets.shape[-2], targets.shape[-1])
    full_attn, w_read, latent_full = (
        lax.all_gather(attn_weights, "fsdp", axis=1, tiled=True),
        lax.all_gather(read_weight, "fsdp", axis=0, tiled=True),
        lax.all_gather(latents, "fsdp", axis=0, tiled=True),
    )
    w_query, w_key, w_value, w_out = (full_attn[0], full_attn[1], full_attn[2], full_attn[3])
    got_tokens, got_counts = (
        lax.all_to_all(
            tokens.reshape(group_size, slot_count, model_width),
            "dp",
            split_axis=0,
            concat_axis=0,
            tiled=True,
        ),
        lax.all_to_all(sent_counts, "dp", split_axis=0, concat_axis=0, tiled=True),
    )
    got_tokens = got_tokens.reshape(event_total, model_width)
    normed, factor, key_rows, value_rows = event_front(got_tokens, w_key, w_value)
    live_slots = live_mask(got_counts, slot_count)
    grad_keys, grad_values, grad_wquery, grad_wout, grad_wread, grad_lat = latent_side(
        latent_full, key_rows, value_rows, live_slots, target, w_query, w_out, w_read
    )
    grad_wkey, grad_wvalue, grad_tokens = event_back(
        got_tokens, factor, normed, grad_keys, grad_values, w_key, w_value
    )
    event_grad = lax.all_to_all(
        grad_tokens.reshape(group_size, slot_count, model_width),
        "dp",
        split_axis=0,
        concat_axis=0,
        tiled=True,
    )
    grad_stack = jnp.stack([grad_wquery, grad_wkey, grad_wvalue, grad_wout])
    owned = (
        lax.psum_scatter(
            grad_stack.astype(jnp.bfloat16), "fsdp", scatter_dimension=1, tiled=True
        ).astype(jnp.float32),
        lax.psum_scatter(
            grad_wread.astype(jnp.bfloat16), "fsdp", scatter_dimension=0, tiled=True
        ).astype(jnp.float32),
        lax.psum_scatter(
            grad_lat.astype(jnp.bfloat16), "fsdp", scatter_dimension=0, tiled=True
        ).astype(jnp.float32),
    )
    summed = (
        lax.psum(owned[0].astype(jnp.bfloat16), "dp").astype(jnp.float32),
        lax.psum(owned[1].astype(jnp.bfloat16), "dp").astype(jnp.float32),
        lax.psum(owned[2].astype(jnp.bfloat16), "dp").astype(jnp.float32),
    )
    return (event_grad.reshape(unit_ids.shape + (model_width,)), summed[0], summed[1], summed[2])


def solution(mesh):
    placed = (
        P("fsdp", "dp", None, None),
        P("fsdp", "dp", None, None),
        P("fsdp", "dp", None),
        P("fsdp", "dp", None, None),
        P(),
        P(),
        P(None, "fsdp", None),
        P("fsdp", None),
        P("fsdp", None),
    )
    return jax.shard_map(
        on_device,
        mesh=mesh,
        in_specs=placed,
        out_specs=(
            P("fsdp", "dp", None, None, None),
            P(None, "fsdp", None),
            P("fsdp", None),
            P("fsdp", None),
        ),
        check_vma=False,
    )
```

profile of v0, /device:TPU:0, one launch (start us, length us, event | category | flops | bytes accessed | tf_op | source)
XLA Modules:
  0.0 503.6 jit_solution(14183431881644624203)
XLA Ops:
  7.2 0.0 all-gather.3.cloned.1.call-start
  7.2 0.7 all-gather.3.cloned.1.call-update
  7.9 1.3 copy.55
  9.2 5.2 %all-to-all-start.1 = ((s32[8,1,1]{2,1,0:T(1,128)}), s32[8,1,1]{2,1,0:T(1,128)S(1)}, u32[]{:S(2)}, u32[]{:S(2)}) async-start(s32[8,1,1]{2,1,0:T(1,128)} %copy.55), calls=%async_computation.1 | async-start | bytes 8192 | tf_op jit(solution)/shard_map/all_to_all | solution.py:148
  14.4 0.8 reshape.181
  15.2 0.8 reshape.180
  15.9 0.8 eq.15
  16.7 4.4 gather_fusion
  21.2 1.1 fusion.28
  22.3 4.3 all-to-all-start
  26.6 0.7 all-gather.5.cloned.1.call-update
  27.3 0.0 reduce-scatter.8.cloned.1.call-start
  27.4 23.2 %all_gather.9 = bf16[256,1024]{1,0:T(8,128)(2,1)S(1)} all-gather(bf16[64,1024]{1,0:T(8,128)(2,1)S(1)} %copy-done.15), channel_id=1, replica_groups=mesh['dp'=8,'fsdp'=4] {'fsdp'}, dimensions={0}, use_global_device_ids=true | all-gather | bytes 655360 | tf_op jit(solution)/shard_map/all_gather | solution.py:137
  50.6 0.2 reduce.1
  50.8 0.1 iota_compare_fusion.2
  50.9 0.1 lt.51
  51.0 0.2 fusion.46
  51.2 0.2 fusion.47
  51.3 119.0 %all-gather.3.cloned.1.call-done = bf16[4,1024,1024]{2,1,0:T(8,128)(2,1)} async-done(((bf16[4,256,1024]{2,1,0:T(8,128)(2,1)}), bf16[4,1024,1024]{2,1,0:T(8,128)(2,1)}) %all-gather.3.cloned.1.call-update) | async-done | bytes 8388624 | tf_op jit(solution)/shard_map/all_gather | solution.py:135
  170.3 2.3 fusion.36
  172.7 3.1 fusion.37
  175.8 2.4 fusion.38
  178.1 0.2 copy.54
  178.3 0.2 copy.57
  178.6 1.4 copy.56
  180.0 3.9 fusion.65
  183.9 2.7 convolution_convert_fusion.2
  186.6 2.4 multiply_reduce_fusion.2
  189.0 9.0 %all-gather.5.cloned.1.call-done = bf16[1024,512]{1,0:T(8,128)(2,1)} async-done(((bf16[256,512]{1,0:T(8,128)(2,1)}), bf16[1024,512]{1,0:T(8,128)(2,1)}) %all-gather.5.cloned.1.call-update) | async-done | bytes 1048592 | tf_op jit(solution)/shard_map/all_gather | solution.py:136
  198.1 2.0 fusion.45
  200.1 0.6 multiply_reduce_fusion.1
  200.6 0.2 multiply_subtract_fusion
  200.9 1.0 copy-done.4
  201.9 3.2 fusion.35
  205.0 2.0 copy.59
  207.1 3.9 fusion.66
  211.0 8.1 %fusion.32 = bf16[16,64,256]{2,1,0:T(8,128)(2,1)} fusion(bf16[256,16,64]{0,2,1:T(8,128)(2,1)} %bitcast.133, f32[16,256,256]{1,2,0:T(8,128)} %fusion.66, f32[16,256,256]{1,2,0:T(8,128)} %get-tuple-element.26, f32[16,256]{1,0:T(8,128)S(1)} %get-tuple-element.25), kind=kOutput, calls=%fused_computation.41 | convolution fusion | flops 141824256 | bytes 9453568 | tf_op jit(solution)/shard_map/hqk,khd->qhd/dot_general | solution.py:26
  219.1 3.6 fusion.39
  222.7 0.0 reduce-scatter.6.cloned.1.call-start
  222.8 1.6 convolution_convert_fusion
  224.3 3.2 convolution_convert_fusion.1
  227.5 0.3 reduce-scatter.4.cloned.1.call-start
  227.8 2.0 convert_bitcast_fusion.3
  229.8 2.0 convert_bitcast_fusion.1
  231.9 7.5 %fusion.29 = bf16[16,64,256]{2,1,0:T(8,128)(2,1)S(1)} fusion(bf16[256,16,64]{0,2,1:T(8,128)(2,1)} %bitcast.131, f32[16,256,256]{1,2,0:T(8,128)} %fusion.66, f32[16,256,256]{1,2,0:T(8,128)} %get-tuple-element.26, f32[16,256]{1,0:T(8,128)S(1)} %get-tuple-element.25), kind=kOutput, calls=%fused_computation.40 | convolution fusion | flops 141824256 | bytes 9453568 | tf_op jit(solution)/shard_map/hqk,qhd->khd/dot_general | solution.py:26
  239.4 0.7 convert_bitcast_fusion.2
  240.1 0.8 convert_bitcast_fusion
  240.9 0.3 copy-done.2
  241.2 0.6 copy-done.3
  241.8 3.8 pad_maximum_fusion
  245.7 0.0 all-reduce.3.cloned.1.call-start
  245.7 0.1 rsqrt.27
  245.8 0.9 copy-done.14
  246.7 2.3 fusion.19
  249.1 22.6 %reduce-scatter.6.cloned.1.call-done = bf16[256,512]{1,0:T(8,128)(2,1)} async-done(((bf16[1024,512]{1,0:T(8,128)(2,1)}), bf16[256,512]{1,0:T(8,128)(2,1)}) %reduce-scatter.6.cloned.1.call-update) | async-done | bytes 262160 | tf_op jit(solution)/shard_map/reduce_scatter | solution.py:171
  271.6 145.5 %reduce-scatter.4.cloned.1.call-done = bf16[4,256,1024]{1,2,0:T(8,128)(2,1)} async-done(((bf16[4,1024,1024]{1,2,0:T(8,128)(2,1)}), bf16[4,256,1024]{1,2,0:T(8,128)(2,1)}) %reduce-scatter.4.cloned.1.call-update) | async-done | bytes 2097168 | tf_op jit(solution)/shard_map/reduce_scatter | solution.py:168
  417.2 2.5 fusion.51
  419.6 0.3 fusion.50
  419.9 16.6 %all_to_all.19 = bf16[8,32,1024]{2,1,0:T(8,128)(2,1)S(1)} all-to-all(bf16[8,32,1024]{2,1,0:T(8,128)(2,1)S(1)} %bitcast.126), channel_id=1, replica_groups=mesh['dp'=8,'fsdp'=4] {'dp'}, dimensions={0} | all-to-all | bytes 1048576 | tf_op jit(solution)/shard_map/all_to_all | solution.py:159
  436.5 51.8 %all-reduce.3.cloned.1.call-done = (bf16[4,256,1024]{1,2,0:T(8,128)(2,1)}, bf16[256,512]{1,0:T(8,128)(2,1)}, bf16[64,1024]{1,0:T(8,128)(2,1)}) async-done(((bf16[4,256,1024]{1,2,0:T(8,128)(2,1)}, bf16[256,512]{1,0:T(8,128)(2,1)}, bf16[64,1024]{1,0:T(8,128)(2,1)}), (bf16[4,256,1024]{1,2,0:T(8,128)(2,1)}, bf16[256,512]{1,0:T(8,128)(2,1)}, bf16[64,1024]{1,0:T(8,128)(2,1)})) %all-reduce.3.cloned.1.call-update) | async-done | bytes 2490384 | tf_op jit(solution)/shard_map/psum | solution.py:179
  488.4 1.7 convert_element_type.169
  490.0 1.8 convert_element_type.167
  491.9 4.1 copy.66
  496.0 0.8 copy.78
  (44 shorter events, 0.3 us)
Async XLA Ops:
  7.2 14.0 %copy-start = (bf16[64,1024]{1,0:T(8,128)(2,1)S(1)}, bf16[64,1024]{1,0:T(8,128)(2,1)}, u32[]{:S(2)}) copy-start(bf16[64,1024]{1,0:T(8,128)(2,1)} %param.14) | copy-start | bytes 393220
  7.2 20.2 %copy-start.15 = (bf16[64,1024]{1,0:T(8,128)(2,1)S(1)}, bf16[64,1024]{1,0:T(8,128)(2,1)}, u32[]{:S(2)}) copy-start(bf16[64,1024]{1,0:T(8,128)(2,1)} %param.17) | copy-start | bytes 393220
  7.2 163.2 %all-gather.3.cloned.1.call-start = ((), (), s32[]{:S(2)}) async-start(), calls=%async_computation.6 | async-start | bytes 10485760 | tf_op jit(solution)/shard_map/all_gather | solution.py:135
  9.2 13.1 %all-to-all-start.1 = ((s32[8,1,1]{2,1,0:T(1,128)}), s32[8,1,1]{2,1,0:T(1,128)S(1)}, u32[]{:S(2)}, u32[]{:S(2)}) async-start(s32[8,1,1]{2,1,0:T(1,128)} %copy.55), calls=%async_computation.1 | async-start | bytes 8192 | tf_op jit(solution)/shard_map/all_to_all | solution.py:148
  22.3 28.6 %all-to-all-start = ((bf16[8,32,1024]{2,1,0:T(8,128)(2,1)}), bf16[8,32,1024]{2,1,0:T(8,128)(2,1)S(1)}, u32[]{:S(2)}, u32[]{:S(2)}) async-start(bf16[8,32,1024]{2,1,0:T(8,128)(2,1)} %bitcast.1), calls=%async_computation | async-start | bytes 1048576 | tf_op jit(solution)/shard_map/all_to_all | solution.py:141
  26.6 171.5 %all-gather.5.cloned.1.call-start = ((), (), s32[]{:S(2)}) async-start(), calls=%async_computation.7 | async-start | bytes 1310720 | tf_op jit(solution)/shard_map/all_gather | solution.py:136
  27.3 221.7 %reduce-scatter.8.cloned.1.call-start = ((), (), s32[]{:S(2)}) async-start(), calls=%async_computation.10 | async-start | bytes 655360 | tf_op jit(solution)/shard_map/reduce_scatter | solution.py:174
  178.3 5.6 %copy-start.10 = (bf16[256,1024]{0,1:T(8,128)(2,1)}, bf16[256,1024]{0,1:T(8,128)(2,1)S(1)}, u32[]{:S(2)}) copy-start(bf16[256,1024]{0,1:T(8,128)(2,1)S(1)} %copy.54) | copy-start | bytes 1572868
  178.6 5.4 %copy-start.6 = (bf16[256,1024]{0,1:T(8,128)(2,1)}, bf16[256,1024]{0,1:T(8,128)(2,1)S(1)}, u32[]{:S(2)}) copy-start(bf16[256,1024]{0,1:T(8,128)(2,1)S(1)} %copy.57) | copy-start | bytes 1572868
  180.0 3.9 copy-start.11
  198.1 2.0 copy-start.9
  200.9 1.0 copy-start.4
  222.7 48.9 %reduce-scatter.6.cloned.1.call-start = ((), (), s32[]{:S(2)}) async-start(), calls=%async_computation.9 | async-start | bytes 1310720 | tf_op jit(solution)/shard_map/reduce_scatter | solution.py:171
  224.3 3.5 copy-start.12
  227.5 2.3 copy-start.7
  227.5 189.6 %reduce-scatter.4.cloned.1.call-start = ((), (), s32[]{:S(2)}) async-start(), calls=%async_computation.8 | async-start | bytes 10485760 | tf_op jit(solution)/shard_map/reduce_scatter | solution.py:168
  231.9 8.3 %copy-start.5 = (f32[256,1024]{1,0:T(8,128)S(1)}, f32[256,1024]{1,0:T(8,128)}, u32[]{:S(2)}) copy-start(f32[256,1024]{1,0:T(8,128)} %copy-done.4) | copy-start | bytes 3145732
  239.4 6.3 %copy-start.13 = (bf16[16,64,256]{2,1,0:T(8,128)(2,1)}, bf16[16,64,256]{2,1,0:T(8,128)(2,1)S(1)}, u32[]{:S(2)}) copy-start(bf16[16,64,256]{2,1,0:T(8,128)(2,1)S(1)} %fusion.29) | copy-start | bytes 1572868
  239.4 1.8 copy-start.2
  239.4 2.4 copy-start.3
  245.6 1.0 copy-start.14
  245.7 171.5 %copy-start.8 = (bf16[16,64,256]{2,1,0:T(8,128)(2,1)S(1)}, bf16[16,64,256]{2,1,0:T(8,128)(2,1)}, u32[]{:S(2)}) copy-start(bf16[16,64,256]{2,1,0:T(8,128)(2,1)} %copy-done.7) | copy-start | bytes 1572868
  245.7 242.7 %all-reduce.3.cloned.1.call-start = ((), (), s32[]{:S(2)}) async-start(), calls=%async_computation.11 | async-start | bytes 4980736 | tf_op jit(solution)/shard_map/psum | solution.py:179
  488.4 8.4 %copy-start.1 = (bf16[64,1024]{1,0:T(8,128)(2,1)S(1)}, bf16[64,1024]{1,0:T(8,128)(2,1)}, u32[]{:S(2)}) copy-start(bf16[64,1024]{1,0:T(8,128)(2,1)} %param.14) | copy-start | bytes 393220
Sparse Core Ops, SparseCore 0:
  9.6 160.7 all-gather.2
  171.9 26.1 all-gather.4
  222.8 21.1 reduce-scatter.7
  246.2 25.4 reduce-scatter.5
  274.0 143.1 reduce-scatter.3
  420.9 67.3 all-reduce.2
where the time goes:
time: 505 us; the launch traced here: 504 us
  waiting for transfers between devices  349 us (69%)
  matrix products  61.8 us (12%)
  blocking collectives  39.8 us (8%)
  local copies, waits for them, and re-layouts  19.8 us (4%)
  between operations  14.4 us (3%)
  starting transfers between devices  9.9 us (2%)
  other arithmetic  8.51 us (2%)
    reduce_scatter x1, waiting for transfers between devices, on_device(): lax.psum_scatter(grad_stack.astype(jnp.bfloat16), 'fsdp', scatter_dimensi...  146 us
    all_gather x1, waiting for transfers between devices, on_device(): lax.all_gather(attn_weights, 'fsdp', axis=1, tiled=True)  119 us
    psum x1, waiting for transfers between devices, on_device(): lax.psum(owned[0].astype(jnp.bfloat16), 'dp').astype(jnp.float32)  51.8 us
    dot_general x16, matrix products, matmul(): return jnp.dot(left, right, preferred_element_type=jnp.float32)  32.5 us
    dot_general x5, matrix products, contract(): return jnp.einsum(form, left, right, preferred_element_type=jnp.float32)  25.4 us
    all_gather x1, blocking collectives, on_device(): lax.all_gather(latents, 'fsdp', axis=0, tiled=True)  23.2 us
    reduce_scatter x1, waiting for transfers between devices, on_device(): lax.psum_scatter(grad_wread.astype(jnp.bfloat16), 'fsdp', scatter_dimensi...  22.6 us
    all_to_all x1, blocking collectives, on_device(): lax.all_to_all(grad_tokens.reshape(group_size, slot_count, model_width),...  16.6 us
  transfers between devices with their start and end apart: 8, of which 5 were waited for; matrix products, arithmetic and copies ran while one was open for 11% of the time, Pallas kernels for 0%

commit v1 on v0

v1 whole, which is shorter than its diff:
```python
import functools

import jax
import jax.numpy as jnp
from jax import lax
from jax.experimental import pallas as pl
from jax.experimental.pallas import tpu as pltpu
from jax.sharding import PartitionSpec as P

HEADS = 16
MESH = pl.DeviceIdType.MESH
MIB = 1 << 20


def flip(index, mask):
    out, bit = index, 1
    while bit <= mask:
        if mask & bit:
            out = out + bit - 2 * bit * lax.rem(lax.div(index, bit), 2)
        bit *= 2
    return out


def bit_orders(n_dp):
    bits = n_dp.bit_length() - 1
    high = [1 << b for b in range(bits - 1, 0, -1)]
    return (high + [1], high[::-1] + [1])


def masks_of(bits):
    out = [0]
    for bit in bits:
        out = out + [mask | bit for mask in out]
    return out


def wait_for(dst, sem):
    pltpu.make_async_copy(dst, dst, sem).wait()


def greet(n_dp, n_f):
    me, mine = lax.axis_index("dp"), lax.axis_index("fsdp")
    barrier = pltpu.get_barrier_semaphore()
    for k in range(1, n_dp):
        pl.semaphore_signal(
            barrier, inc=1, device_id={"dp": lax.rem(me + k, n_dp)}, device_id_type=MESH
        )
    for k in range(1, n_f):
        pl.semaphore_signal(
            barrier, inc=1, device_id={"fsdp": lax.rem(mine + k, n_f)}, device_id_type=MESH
        )
    pl.semaphore_wait(barrier, n_dp + n_f - 2)


def exchange_start(n_dp, src, dst, send, recv, local):
    me = lax.axis_index("dp")
    copies = []
    for k in range(1, n_dp):
        to = lax.rem(me + k, n_dp)
        copy = pltpu.make_async_remote_copy(
            src_ref=src.at[to],
            dst_ref=dst.at[me],
            send_sem=send.at[k],
            recv_sem=recv.at[k],
            device_id={"dp": to},
            device_id_type=MESH,
        )
        copy.start()
        copies.append(copy)
    own = pltpu.make_async_copy(src.at[me], dst.at[me], local)
    own.start()
    return copies, own


def exchange_finish(n_dp, started, dst, recv):
    me = lax.axis_index("dp")
    copies, own = started
    for k in range(1, n_dp):
        wait_for(dst.at[lax.rem(me + n_dp - k, n_dp)], recv.at[k])
    for copy in copies:
        copy.wait_send()
    own.wait()


def doubling(order, n_dp, half, buf, send, recv, ready):
    me = lax.axis_index("dp")
    held, copies, number = [0], [], 0
    for stage, bit in enumerate(order):
        for mask in held:
            if mask == 0:
                if stage == 0:
                    ready()
            elif mask & order[stage - 1]:
                wait_for(buf(flip(me, mask)), recv.at[half, mask])
            piece = buf(flip(me, mask))
            copy = pltpu.make_async_remote_copy(
                src_ref=piece,
                dst_ref=piece,
                send_sem=send.at[half, number],
                recv_sem=recv.at[half, mask | bit],
                device_id={"dp": flip(me, bit)},
                device_id_type=MESH,
            )
            copy.start()
            copies.append(copy)
            number += 1
        held = held + [mask | bit for mask in held]
        yield True
    for mask in held:
        if mask & order[-1]:
            wait_for(buf(flip(me, mask)), recv.at[half, mask])
    for copy in copies:
        copy.wait_send()


def staggered(walks):
    waiting, active = list(walks), []
    while waiting or active:
        if waiting:
            active.append(waiting.pop(0))
        still = []
        for walk in active:
            if next(walk, None) is not None:
                still.append(walk)
        active = still


def gather_kernel(n_dp, n_f, halves, ids, shard, got_ids, full, id_send, id_recv, z_send, send, recv, local):
    me, mine = lax.axis_index("dp"), lax.axis_index("fsdp")
    greet(n_dp, n_f)
    started = exchange_start(n_dp, ids, got_ids, id_send, id_recv, local.at[0])
    z_copies = []

    def send_over(half):
        for k in range(1, n_f):
            copy = pltpu.make_async_remote_copy(
                src_ref=shard.at[me, half],
                dst_ref=full.at[mine, me, half],
                send_sem=z_send.at[half, k],
                recv_sem=recv.at[n_f - k, half, 0],
                device_id={"fsdp": lax.rem(mine + k, n_f)},
                device_id_type=MESH,
            )
            copy.start()
            z_copies.append(copy)

    for half in range(min(2, halves)):
        send_over(half)
    own = pltpu.make_async_copy(shard, full.at[mine], local.at[1])
    own.start()
    orders = bit_orders(n_dp)

    def lane(half):
        walks = []
        for r in range(1, n_f):
            owner = lax.rem(mine + r, n_f)

            def buf(d, owner=owner):
                return full.at[owner, d, half]

            def ready(buf=buf, r=r):
                wait_for(buf(me), recv.at[r, half, 0])

            walks.append(
                doubling(orders[half % 2], n_dp, half, buf, send.at[r], recv.at[r], ready)
            )
        if half + 2 < halves:
            send_over(half + 2)
        for _ in orders[half % 2]:
            for walk in walks:
                next(walk)
            yield True
        for walk in walks:
            next(walk, None)

    staggered([lane(half) for half in range(halves)])
    for copy in z_copies:
        copy.wait_send()
    own.wait()
    exchange_finish(n_dp, started, got_ids, id_recv)


def gather_params(n_dp, n_f, ids, shard):
    halves = shard.shape[1]
    return pl.pallas_call(
        functools.partial(gather_kernel, n_dp, n_f, halves),
        out_shape=(
            jax.ShapeDtypeStruct(ids.shape, ids.dtype),
            jax.ShapeDtypeStruct((n_f,) + shard.shape, shard.dtype),
        ),
        in_specs=[pl.BlockSpec(memory_space=pltpu.VMEM)] * 2,
        out_specs=[pl.BlockSpec(memory_space=pltpu.VMEM)] * 2,
        scratch_shapes=[
            pltpu.SemaphoreType.DMA((n_dp,)),
            pltpu.SemaphoreType.DMA((n_dp,)),
            pltpu.SemaphoreType.DMA((halves, n_f)),
            pltpu.SemaphoreType.DMA((n_f, halves, n_dp)),
            pltpu.SemaphoreType.DMA((n_f, halves, n_dp)),
            pltpu.SemaphoreType.DMA((2,)),
        ],
        compiler_params=pltpu.CompilerParams(
            collective_id=0, has_side_effects=True, vmem_limit_bytes=40 * MIB
        ),
    )(ids, shard)


def halving(order, n_dp, half, grads, out_buf, in_buf, send, recv, load_sem):
    me = lax.axis_index("dp")
    n_f = grads.shape[0]
    bits, copies, number = order[::-1], [], 0
    pending, loaded = [], set()

    def load(mask):
        if mask not in loaded:
            loaded.add(mask)
            wait_for(grads.at[:, flip(me, mask), half], load_sem.at[half, mask])

    def add(slot, mask):
        load(mask)
        wait_for(in_buf.at[half, slot], recv.at[half, slot])
        where = flip(me, mask)
        for f in range(n_f):
            grads[f, where, half] += in_buf[half, slot, f].astype(jnp.float32)

    for stage, bit in enumerate(bits):
        rest = masks_of(bits[stage + 1:][::-1])
        rest = sorted(rest, key=lambda m: 0 if stage + 1 < len(bits) and m & bits[stage + 1] else 1)
        sends = [bit | m for m in rest]
        arrived = dict(pending)
        for mask in sends:
            if mask in arrived:
                add(arrived.pop(mask), mask)
            load(mask)
            slot = number
            number += 1
            where = flip(me, mask)
            for f in range(n_f):
                out_buf[half, slot, f] = grads[f, where, half].astype(jnp.bfloat16)
            copy = pltpu.make_async_remote_copy(
                src_ref=out_buf.at[half, slot],
                dst_ref=in_buf.at[half, slot],
                send_sem=send.at[half, slot],
                recv_sem=recv.at[half, slot],
                device_id={"dp": flip(me, bit)},
                device_id_type=MESH,
            )
            copy.start()
            copies.append(copy)
        yield True
        for mask, slot in arrived.items():
            add(slot, mask)
        pending = [(m, number - len(sends) + n) for n, m in enumerate(rest)]
    for mask, slot in pending:
        add(slot, mask)
    for copy in copies:
        copy.wait_send()


def reduce_kernel(
    n_dp, n_f, halves, source, events, summed, got_events, grads, out_buf, in_buf, z_out, z_in,
    load_sem, ev_send, ev_recv, h_send, h_recv, z_send, z_recv, d_send, d_recv, local,
):
    me, mine = lax.axis_index("dp"), lax.axis_index("fsdp")
    greet(n_dp, n_f)
    orders = bit_orders(n_dp)
    for half in range(halves):
        for mask in sorted(range(n_dp), key=lambda m: 0 if m & 1 else 1):
            where = flip(me, mask)
            pltpu.make_async_copy(
                source.at[:, where, half], grads.at[:, where, half], load_sem.at[half, mask]
            ).start()
    started = exchange_start(n_dp, events, got_events, ev_send, ev_recv, local.at[0])
    z_copies = []

    def lane(half):
        order = orders[half % 2]
        yield from halving(
            order, n_dp, half, grads, out_buf, in_buf, h_send, h_recv, load_sem
        )
        for k in range(1, n_f):
            to = lax.rem(mine + k, n_f)
            z_out[half, k] = grads[to, me, half].astype(jnp.bfloat16)
            copy = pltpu.make_async_remote_copy(
                src_ref=z_out.at[half, k],
                dst_ref=z_in.at[half, k],
                send_sem=z_send.at[half, k],
                recv_sem=z_recv.at[half, k],
                device_id={"fsdp": to},
                device_id_type=MESH,
            )
            copy.start()
            z_copies.append(copy)
        yield True

        def ready():
            total = grads[mine, me, half]
            for k in range(1, n_f):
                wait_for(z_in.at[half, k], z_recv.at[half, k])
                total = total + z_in[half, k].astype(jnp.float32)
            summed[me, half] = total.astype(jnp.bfloat16)

        def buf(d):
            return summed.at[d, half]

        yield from doubling(order, n_dp, half, buf, d_send, d_recv, ready)

    staggered([lane(half) for half in range(halves)])
    for copy in z_copies:
        copy.wait_send()
    exchange_finish(n_dp, started, got_events, ev_recv)


def reduce_grads(n_dp, n_f, grads, events):
    halves, rows, width = grads.shape[-3:]
    low = jnp.bfloat16
    return pl.pallas_call(
        functools.partial(reduce_kernel, n_dp, n_f, halves),
        out_shape=(
            jax.ShapeDtypeStruct(grads.shape[1:], low),
            jax.ShapeDtypeStruct(events.shape, low),
        ),
        in_specs=[pl.BlockSpec(memory_space=pl.ANY)] * 2,
        out_specs=[pl.BlockSpec(memory_space=pltpu.VMEM), pl.BlockSpec(memory_space=pl.ANY)],
        scratch_shapes=[
            pltpu.VMEM(grads.shape, jnp.float32),
            pltpu.VMEM((halves, n_dp - 1, n_f, rows, width), low),
            pltpu.VMEM((halves, n_dp - 1, n_f, rows, width), low),
            pltpu.VMEM((halves, n_f, rows, width), low),
            pltpu.VMEM((halves, n_f, rows, width), low),
            pltpu.SemaphoreType.DMA((halves, n_dp)),
            pltpu.SemaphoreType.DMA((n_dp,)),
            pltpu.SemaphoreType.DMA((n_dp,)),
            pltpu.SemaphoreType.DMA((halves, n_dp)),
            pltpu.SemaphoreType.DMA((halves, n_dp)),
            pltpu.SemaphoreType.DMA((halves, n_f)),
            pltpu.SemaphoreType.DMA((halves, n_f)),
            pltpu.SemaphoreType.DMA((halves, n_dp)),
            pltpu.SemaphoreType.DMA((halves, n_dp)),
            pltpu.SemaphoreType.DMA((1,)),
        ],
        compiler_params=pltpu.CompilerParams(
            collective_id=1, has_side_effects=True, vmem_limit_bytes=60 * MIB
        ),
    )(grads, events)


eps = 1e-05


def rms_scale(rows):
    return lax.rsqrt(jnp.mean(rows * rows, axis=-1, keepdims=True) + eps)


def rms_back(rows, factor, grad_out):
    cubed = factor * factor * factor
    return factor * grad_out - rows * cubed * jnp.mean(grad_out * rows, axis=-1, keepdims=True)


def dot_nn(left, right):
    return lax.dot_general(left, right, (((1,), (0,)), ((), ())), preferred_element_type=jnp.float32)


def dot_nt(left, right):
    return lax.dot_general(left, right, (((1,), (1,)), ((), ())), preferred_element_type=jnp.float32)


def dot_tn(left, right):
    return lax.dot_general(left, right, (((0,), (0,)), ((), ())), preferred_element_type=jnp.float32)


def window_kernel(
    sizes, slots, full, unit_table, session_table, target, grads, grad_tokens,
    tokens, normed, keys, values, query, mixed, gmixed, gquery, gkeys, gvalues, lat, lnorm, peak, scale,
    resid, ring, sems,
):
    n_f, own, read_rows, lat_rows, out_width = sizes
    width = tokens.shape[1]
    low = jnp.bfloat16
    base_read = 4 * own
    base_lat = base_read + read_rows
    end = base_lat + lat_rows
    times = width // out_width
    W_Q, W_K, W_V, W_O = range(4)
    state = {"n": 0, "busy": [None] * ring.shape[0]}

    def put(f, row, value):
        slot = state["n"] % ring.shape[0]
        state["n"] += 1
        if state["busy"][slot] is not None:
            state["busy"][slot].wait()
        rows = value.shape[0]
        ring[slot, pl.ds(0, rows)] = value
        copy = pltpu.make_async_copy(
            ring.at[slot, pl.ds(0, rows)], grads.at[f, pl.ds(row, rows)], sems.at[slot]
        )
        copy.start()
        state["busy"][slot] = copy

    def cols(f):
        return slice(f * own, (f + 1) * own)

    def block(k, f):
        return full[f, k * own:(k + 1) * own]

    def times_weight(left, k):
        total = dot_nn(left[:, cols(0)], block(k, 0))
        for f in range(1, n_f):
            total = total + dot_nn(left[:, cols(f)], block(k, f))
        return total

    def grad_matrix(left, right, k):
        for f in range(n_f):
            put(f, k * own, dot_tn(left[:, cols(f)], right[...]))

    slots_unit, slots_session, live = slots[0:1], slots[1:2], slots[2:3] > 0
    events = tokens.shape[0]

    def pick(table, ids, start, count):
        at = lax.broadcasted_iota(jnp.int32, (count, events), 0) + start
        return dot_tn((at == ids).astype(low), table[start:start + count])

    unit_rows = unit_table.shape[0]
    step = min(512, unit_rows)
    total = pick(unit_table, slots_unit, 0, step)
    for start in range(step, unit_rows, step):
        total = total + pick(unit_table, slots_unit, start, min(step, unit_rows - start))
    total = total + pick(session_table, slots_session, 0, session_table.shape[0])
    tokens[...] = total.astype(low)
    rows = tokens[...].astype(jnp.float32)
    normed[...] = (rows * rms_scale(rows)).astype(low)
    keys[...] = times_weight(normed, W_K).astype(low)
    values[...] = times_weight(normed, W_V).astype(low)
    for f in range(n_f):
        lat[f * lat_rows:(f + 1) * lat_rows] = full[f, base_lat:end]
    query[...] = times_weight(lat, W_Q).astype(low)

    latent_count = lat.shape[0]
    head_dim = width // HEADS
    head_factor = head_dim ** (-0.5)
    pack = 128 // head_dim
    which = lax.broadcasted_iota(jnp.int32, (1, 128), 1) // head_dim

    def masked(rows, part):
        return jnp.where(which == part, rows, jnp.zeros_like(rows))

    def merge(parts):
        out = parts[0]
        for part in range(1, pack):
            out = jnp.where(which == part, parts[part], out)
        return out

    def lanes(p):
        return pl.ds(pl.multiple_of(p * 128, 128), 128)

    def scores_of(q, k, part):
        return jnp.where(live, dot_nt(masked(q, part), k) * head_factor, -1e30)

    def forward(p, carry):
        q, k, v = query[:, lanes(p)], keys[:, lanes(p)], values[:, lanes(p)]
        outs = []
        for part in range(pack):
            s = scores_of(q, k, part)
            top = jnp.max(s, axis=-1, keepdims=True)
            w = jnp.where(live, jnp.exp(s - top), 0.0)
            inverse = 1.0 / jnp.sum(w, axis=-1, keepdims=True)
            peak[p * pack + part] = top
            scale[p * pack + part] = inverse
            outs.append(dot_nn((w * inverse).astype(low), v))
        mixed[:, lanes(p)] = merge(outs).astype(low)
        return carry

    lax.fori_loop(0, width // 128, forward, 0)

    resid[...] = lat[...].astype(jnp.float32) + times_weight(mixed, W_O)
    factor = rms_scale(resid[...])
    lnorm[...] = (resid[...] * factor).astype(low)

    def pieces():
        step = own // times
        for f in range(n_f):
            for t in range(times):
                at = f * own + t * step
                yield f, t, slice(at, at + step), full[f, base_read:base_lat, t * out_width:(t + 1) * out_width]

    logits = None
    for f, t, at, weight in pieces():
        term = dot_nn(lnorm[:, at], weight)
        logits = term if logits is None else logits + term
    glogits = (
        (jax.nn.sigmoid(logits) - target[...].astype(jnp.float32)) * latent_count ** (-0.5)
    ).astype(low)
    for f in range(n_f):
        put(f, base_read, jnp.concatenate(
            [dot_tn(lnorm[:, at], glogits) for g, t, at, _ in pieces() if g == f], axis=1
        ))
    glnorm = jnp.concatenate([dot_nt(glogits, weight) for _, _, _, weight in pieces()], axis=1)
    gresid = rms_back(resid[...], factor, glnorm)
    resid[...] = gresid
    gresid_low = gresid.astype(low)
    for f in range(n_f):
        gmixed[:, cols(f)] = dot_nt(gresid_low, block(W_O, f)).astype(low)
    lnorm[...] = gresid_low
    grad_matrix(mixed, lnorm, W_O)

    def backward(p, carry):
        q, k, v, g = query[:, lanes(p)], keys[:, lanes(p)], values[:, lanes(p)], gmixed[:, lanes(p)]
        outs = ([], [], [])
        for part in range(pack):
            s = scores_of(q, k, part)
            probs = jnp.where(live, jnp.exp(s - peak[p * pack + part]), 0.0) * scale[p * pack + part]
            gprobs = dot_nt(masked(g, part), v)
            inner = jnp.sum(gprobs * probs, axis=-1, keepdims=True)
            gscores = (probs * (gprobs - inner) * head_factor).astype(low)
            outs[0].append(dot_tn(probs.astype(low), g))
            outs[1].append(dot_nn(gscores, k))
            outs[2].append(dot_tn(gscores, q))
        gvalues[:, lanes(p)] = merge(outs[0]).astype(low)
        gquery[:, lanes(p)] = merge(outs[1]).astype(low)
        gkeys[:, lanes(p)] = merge(outs[2]).astype(low)
        return carry

    lax.fori_loop(0, width // 128, backward, 0)

    grad_matrix(lat, gquery, W_Q)
    for f in range(n_f):
        resid[:, cols(f)] += dot_nt(gquery[...], block(W_Q, f))
    for f in range(n_f):
        put(f, base_lat, resid[f * lat_rows:(f + 1) * lat_rows])
    grad_matrix(normed, gkeys, W_K)
    grad_matrix(normed, gvalues, W_V)
    spare = grads.shape[1] - end
    if spare:
        for f in range(n_f):
            put(f, end, jnp.zeros((spare, width), jnp.float32))
    gnormed = jnp.concatenate(
        [
            dot_nt(gkeys[...], block(W_K, f)) + dot_nt(gvalues[...], block(W_V, f))
            for f in range(n_f)
        ],
        axis=1,
    )
    rows = tokens[...].astype(jnp.float32)
    grad_tokens[...] = rms_back(rows, rms_scale(rows), gnormed).astype(low)
    for copy in state["busy"]:
        if copy is not None:
            copy.wait()


def window_grads(sizes, slots, full, unit_table, session_table, target):
    n_f, own, read_rows, lat_rows, out_width = sizes
    events, width = slots.shape[1], full.shape[-1]
    latent_count = n_f * lat_rows
    low = jnp.bfloat16
    spare = full.shape[1] - 4 * own - read_rows - lat_rows
    ring_rows = max(own, spare)
    by_event = pltpu.VMEM((events, width), low)
    by_latent = pltpu.VMEM((latent_count, width), low)
    column = pltpu.VMEM((HEADS, latent_count, 1), jnp.float32)
    return pl.pallas_call(
        functools.partial(window_kernel, sizes),
        out_shape=(
            jax.ShapeDtypeStruct(full.shape, jnp.float32),
            jax.ShapeDtypeStruct((events, width), low),
        ),
        in_specs=[pl.BlockSpec(memory_space=pltpu.VMEM)] * 5,
        out_specs=[pl.BlockSpec(memory_space=pl.ANY), pl.BlockSpec(memory_space=pltpu.VMEM)],
        scratch_shapes=[
            by_event, by_event, by_event, by_event,
            by_latent, by_latent, by_latent, by_latent,
            by_event, by_event, by_latent, by_latent, column, column,
            pltpu.VMEM((latent_count, width), jnp.float32),
            pltpu.VMEM((4, ring_rows, width), jnp.float32),
            pltpu.SemaphoreType.DMA((4,)),
        ],
        compiler_params=pltpu.CompilerParams(vmem_limit_bytes=60 * MIB),
    )(slots, full, unit_table, session_table, target)


def piece_rows(rows, n_dp):
    options = []
    for lanes in range(1, 6):
        lane_rows = -(-rows // (n_dp * lanes * 16)) * 16
        options.append((lane_rows * lanes, -lanes, lane_rows))
    _, lanes, lane_rows = min(options)
    return lane_rows, -lanes


def fold(rows, width):
    times = width // rows.shape[-1]
    step = rows.shape[-2] // times
    return jnp.concatenate(
        [rows[..., k * step:(k + 1) * step, :] for k in range(times)], axis=-1
    )


def unfold(rows, narrow):
    times = rows.shape[-1] // narrow
    return jnp.concatenate(
        [rows[..., k * narrow:(k + 1) * narrow] for k in range(times)], axis=-2
    )


def on_device(
    unit_ids,
    session_ids,
    counts,
    targets,
    unit_table,
    session_table,
    attn_weights,
    read_weight,
    latents,
):
    n_dp, n_f = lax.axis_size("dp"), lax.axis_size("fsdp")
    slot_count = unit_ids.shape[-1]
    width = unit_table.shape[1]
    event_total = n_dp * slot_count
    stack, own_rows, _ = attn_weights.shape
    read_rows = read_weight.size // width
    lat_rows = latents.shape[0]
    out_width = read_weight.shape[1]
    ends = (stack * own_rows, stack * own_rows + read_rows, stack * own_rows + read_rows + lat_rows)
    rows, halves = piece_rows(ends[2], n_dp)
    padded = rows * halves * n_dp

    id_rows = jnp.concatenate(
        [
            unit_ids.reshape(n_dp, slot_count),
            session_ids.reshape(n_dp, slot_count),
            (jnp.arange(slot_count, dtype=jnp.int32) < counts.reshape(n_dp, 1)).astype(jnp.int32),
        ],
        axis=1,
    )
    id_rows = jnp.pad(id_rows, ((0, 0), (0, 128 - id_rows.shape[1]))).reshape(n_dp, 1, 128)
    shard = jnp.concatenate(
        [
            attn_weights.reshape(stack * own_rows, width),
            fold(read_weight, width),
            latents,
            jnp.zeros((padded - ends[2], width), jnp.bfloat16),
        ]
    ).reshape(n_dp, halves, rows, width)
    got_ids, full = gather_params(n_dp, n_f, id_rows, shard)
    full = full.reshape(n_f, padded, width)
    sizes = (n_f, own_rows, read_rows, lat_rows, out_width)
    slots = jnp.transpose(got_ids[:, 0, :3 * slot_count].reshape(n_dp, 3, slot_count), (1, 0, 2))
    grads, grad_tokens = window_grads(
        sizes,
        slots.reshape(3, event_total),
        full,
        unit_table,
        session_table,
        targets.reshape(targets.shape[-2], out_width),
    )
    grads = grads.reshape(n_f, n_dp, halves, rows, width)
    summed, event_grad = reduce_grads(
        n_dp, n_f, grads, grad_tokens.reshape(n_dp, slot_count, width)
    )
    summed = summed.reshape(padded, width)
    return (
        event_grad.reshape(unit_ids.shape + (width,)),
        summed[:ends[0]].reshape(stack, own_rows, width).astype(jnp.float32),
        unfold(summed[ends[0]:ends[1]], out_width).astype(jnp.float32),
        summed[ends[1]:ends[2]].astype(jnp.float32),
    )


def solution(mesh):
    placed = (
        P("fsdp", "dp", None, None),
        P("fsdp", "dp", None, None),
        P("fsdp", "dp", None),
        P("fsdp", "dp", None, None),
        P(),
        P(),
        P(None, "fsdp", None),
        P("fsdp", None),
        P("fsdp", None),
    )
    return jax.shard_map(
        on_device,
        mesh=mesh,
        in_specs=placed,
        out_specs=(
            P("fsdp", "dp", None, None, None),
            P(None, "fsdp", None),
            P("fsdp", None),
            P("fsdp", None),
        ),
        check_vma=False,
    )
```

time: 505 us -> 212 us (0.42)
  waiting for transfers between devices: 349 us -> 0 us
  Pallas kernels: 0 us -> 188 us
  matrix products: 61.8 us -> 0 us
  blocking collectives: 39.8 us -> 0 us
  between operations: 14.4 us -> 0.7 us
  local copies, waits for them, and re-layouts: 19.8 us -> 9.34 us
  starting transfers between devices: 9.9 us -> 0 us
  other arithmetic: 8.51 us -> 13.6 us
    pallas_call x0 -> x3, Pallas kernels: none -> 188 us  [the longest x1 92.6 us: reduce_grads(): pl.pallas_call(functools.partial(reduce_kernel, n_dp, n_f, halves), out_s...]
    reduce_scatter x3 -> x0, waiting for transfers between devices: 168 us -> none  [the longest x1 146 us: on_device(): lax.psum_scatter(grad_stack.astype(jnp.bfloat16), 'fsdp', scatter_dimensi...]
    all_gather x2 -> x0, waiting for transfers between devices: 128 us -> none  [the longest x1 119 us: on_device(): lax.all_gather(attn_weights, 'fsdp', axis=1, tiled=True)]
    dot_general x21 -> x0, matrix products: 57.9 us -> none  [the longest x16 32.5 us: matmul(): return jnp.dot(left, right, preferred_element_type=jnp.float32)]
    psum x1 -> x0, waiting for transfers between devices: 51.8 us -> none  [on_device(): lax.psum(owned[0].astype(jnp.bfloat16), 'dp').astype(jnp.float32)]
    all_gather x1 -> x0, blocking collectives: 23.2 us -> none  [on_device(): lax.all_gather(latents, 'fsdp', axis=0, tiled=True)]
    all_to_all x1 -> x0, blocking collectives: 16.6 us -> none  [on_device(): lax.all_to_all(grad_tokens.reshape(group_size, slot_count, model_width),...]
    all_to_all x2 -> x0, starting transfers between devices: 9.44 us -> none  [the longest x1 5.17 us: on_device(): lax.all_to_all(sent_counts, 'dp', split_axis=0, concat_axis=0, tiled=True)]
  transfers between devices with their start and end apart: 8 -> 0, of which waited for: 5 -> 0; matrix products, arithmetic and copies ran while one was open for 11% -> 0% of each run, Pallas kernels for 0% -> 0%
where the time goes in v1:
time: 212 us
  Pallas kernels  188 us (89%)
  other arithmetic  13.6 us (6%)
  local copies, waits for them, and re-layouts  9.34 us (4%)
    pallas_call x1, Pallas kernels, reduce_grads(): pl.pallas_call(functools.partial(reduce_kernel, n_dp, n_f, halves), out_s...  92.6 us
    pallas_call x1, Pallas kernels, gather_params(): pl.pallas_call(functools.partial(gather_kernel, n_dp, n_f, halves), out_s...  58 us
    pallas_call x1, Pallas kernels, window_grads(): pl.pallas_call(functools.partial(window_kernel, sizes), out_shape=(jax.Sh...  37.8 us
    concatenate x1, other arithmetic, on_device(): jnp.concatenate([attn_weights.reshape(stack * own_rows, width), fold(read...  7.1 us
    unnamed x5, local copies, waits for them, and re-layouts  4.75 us

profile of v1, /device:TPU:0, one launch (start us, length us, event | category | flops | bytes accessed | tf_op | source)
XLA Modules:
  0.0 212.0 jit_solution(11600571849977187551)
XLA Ops:
  0.6 0.1 pad.11.clone
  0.7 0.7 fusion
  1.4 0.8 pad_add_fusion
  2.2 1.0 fusion.2
  3.2 7.1 %maximum_maximum_fusion = bf16[1280,1024]{1,0:T(8,128)(2,1)S(1)} fusion(bf16[64,1024]{1,0:T(8,128)(2,1)} %param.17, bf16[128,512]{1,0:T(8,128)(2,1)S(1)} %get-tuple-element.19, bf16[128,512]{1,0:T(8,128)(2,1)S(1)} %get-tuple-element.18, bf16[1024,1024]{1,0:T(8,128)(2,1)} %bitcast.23, bf16[1280]{0:T(1024)(128)(2,1)S(1)} %pad.11.clone), kind=kLoop, calls=%fused_computation | loop fusion | flops 13107200 | bytes 5114368 | tf_op jit(solution)/shard_map/concatenate | solution.py:635
  10.3 58.0 %shard_map.120 = (s32[8,1,128]{2,1,0:T(1,128)S(1)}, bf16[4,8,5,32,1024]{4,3,2,1,0:T(8,128)(2,1)S(1)}) custom-call(s32[8,1,128]{2,1,0:T(1,128)S(1)} %bitcast.17, bf16[8,5,32,1024]{3,2,1,0:T(8,128)(2,1)S(1)} %bitcast.16), custom_call_target="tpu_custom_call" | custom-call | tf_op jit(solution)/shard_map/pallas_call | solution.py:185
  68.4 0.0 copy-start
  68.4 4.0 %copy-done = bf16[4,8,5,32,1024]{4,3,2,1,0:T(8,128)(2,1)} copy-done((bf16[4,8,5,32,1024]{4,3,2,1,0:T(8,128)(2,1)}, bf16[4,8,5,32,1024]{4,3,2,1,0:T(8,128)(2,1)S(1)}, u32[]{:S(2)}) %copy-start) | copy-done | bytes 10485784
  72.3 0.1 reshape_squeeze.3
  72.4 0.7 reshape.54.slots
  73.1 37.8 %shard_map.121 = (f32[4,1280,1024]{2,1,0:T(8,128)}, bf16[256,1024]{1,0:T(8,128)(2,1)}) custom-call(s32[3,256]{1,0:T(4,128)} %reshape.54.slots, bf16[4,1280,1024]{2,1,0:T(8,128)(2,1)} %bitcast.15, bf16[2048,1024]{1,0:T(8,128)(2,1)} %unit_table.1, bf16[64,1024]{1,0:T(8,128)(2,1)} %session_table.1, s32[256,512]{1,0:T(8,128)} %bitcast.24), custom_call_target="tpu_custom_call" | custom-call | tf_op jit(solution)/shard_map/pallas_call | solution.py:559
  110.9 92.6 %shard_map.122 = (bf16[8,5,32,1024]{3,2,1,0:T(8,128)(2,1)}, bf16[8,32,1024]{2,1,0:T(8,128)(2,1)}) custom-call(f32[4,8,5,32,1024]{4,3,2,1,0:T(8,128)} %bitcast.18, bf16[8,32,1024]{2,1,0:T(8,128)(2,1)} %bitcast.26), custom_call_target="tpu_custom_call" | custom-call | tf_op jit(solution)/shard_map/pallas_call | solution.py:316
  203.5 1.6 slice_convert_fusion
  205.1 1.0 fusion.1
  206.1 1.8 slice.31
  207.9 0.0 copy-start.1
  207.9 0.9 maximum_convert_fusion
  208.7 2.5 %convert.1 = f32[4,256,1024]{2,1,0:T(8,128)} convert(bf16[4,256,1024]{2,1,0:T(8,128)(2,1)S(1)} %bitcast.19) | non-fusion elementwise | flops 1048576 | bytes 6291456 | tf_op jit(solution)/shard_map/convert_element_type | solution.py:662
  211.2 0.0 copy-done.1
  211.2 0.8 copy.16
  (4 shorter events, 0.0 us)
Async XLA Ops:
  68.4 4.0 %copy-start = (bf16[4,8,5,32,1024]{4,3,2,1,0:T(8,128)(2,1)}, bf16[4,8,5,32,1024]{4,3,2,1,0:T(8,128)(2,1)S(1)}, u32[]{:S(2)}) copy-start(bf16[4,8,5,32,1024]{4,3,2,1,0:T(8,128)(2,1)S(1)} %get-tuple-element.11) | copy-start | bytes 31457284
  207.9 3.4 %copy-start.1 = (bf16[8,32,1024]{2,1,0:T(8,128)(2,1)S(1)}, bf16[8,32,1024]{2,1,0:T(8,128)(2,1)}, u32[]{:S(2)}) copy-start(bf16[8,32,1024]{2,1,0:T(8,128)(2,1)} %get-tuple-element.14) | copy-start | bytes 1572868

commit v2 on v1

--- a/solution.py
+++ b/solution.py
@@ -123,19 +123,23 @@
             if next(walk, None) is not None:
                 still.append(walk)
         active = still
-
-
-def gather_kernel(n_dp, n_f, halves, ids, shard, got_ids, full, id_send, id_recv, z_send, send, recv, local):
+        yield True
+
+
+def gather(n_dp, n_f, halves, lane_rows, full, z_send, send, recv):
     me, mine = lax.axis_index("dp"), lax.axis_index("fsdp")
-    greet(n_dp, n_f)
-    started = exchange_start(n_dp, ids, got_ids, id_send, id_recv, local.at[0])
-    z_copies = []
+    z_copies, done = [], set()
+    orders = bit_orders(n_dp)
+
+    def at(d, half):
+        return pl.ds(pl.multiple_of((half * n_dp + d) * lane_rows, 16), lane_rows)
 
     def send_over(half):
         for k in range(1, n_f):
+            piece = full.at[mine, at(me, half)]
             copy = pltpu.make_async_remote_copy(
-                src_ref=shard.at[me, half],
-                dst_ref=full.at[mine, me, half],
+                src_ref=piece,
+                dst_ref=piece,
                 send_sem=z_send.at[half, k],
                 recv_sem=recv.at[n_f - k, half, 0],
                 device_id={"fsdp": lax.rem(mine + k, n_f)},
@@ -146,9 +150,6 @@
 
     for half in range(min(2, halves)):
         send_over(half)
-    own = pltpu.make_async_copy(shard, full.at[mine], local.at[1])
-    own.start()
-    orders = bit_orders(n_dp)
 
     def lane(half):
         walks = []
@@ -156,7 +157,7 @@
             owner = lax.rem(mine + r, n_f)
 
             def buf(d, owner=owner):
-                return full.at[owner, d, half]
+                return full.at[owner, at(d, half)]
 
             def ready(buf=buf, r=r):
                 wait_for(buf(me), recv.at[r, half, 0])
@@ -172,36 +173,22 @@
             yield True
         for walk in walks:
             next(walk, None)
-
-    staggered([lane(half) for half in range(halves)])
-    for copy in z_copies:
-        copy.wait_send()
-    own.wait()
-    exchange_finish(n_dp, started, got_ids, id_recv)
-
-
-def gather_params(n_dp, n_f, ids, shard):
-    halves = shard.shape[1]
-    return pl.pallas_call(
-        functools.partial(gather_kernel, n_dp, n_f, halves),
-        out_shape=(
-            jax.ShapeDtypeStruct(ids.shape, ids.dtype),
-            jax.ShapeDtypeStruct((n_f,) + shard.shape, shard.dtype),
-        ),
-        in_specs=[pl.BlockSpec(memory_space=pltpu.VMEM)] * 2,
-        out_specs=[pl.BlockSpec(memory_space=pltpu.VMEM)] * 2,
-        scratch_shapes=[
-            pltpu.SemaphoreType.DMA((n_dp,)),
-            pltpu.SemaphoreType.DMA((n_dp,)),
-            pltpu.SemaphoreType.DMA((halves, n_f)),
-            pltpu.SemaphoreType.DMA((n_f, halves, n_dp)),
-            pltpu.SemaphoreType.DMA((n_f, halves, n_dp)),
-            pltpu.SemaphoreType.DMA((2,)),
-        ],
-        compiler_params=pltpu.CompilerParams(
-            collective_id=0, has_side_effects=True, vmem_limit_bytes=40 * MIB
-        ),
-    )(ids, shard)
+        done.add(half)
+
+    progress = staggered([lane(half) for half in range(halves)])
+
+    def need(stop):
+        last = -(-stop // (n_dp * lane_rows)) - 1
+        while not all(half in done for half in range(last + 1)):
+            next(progress)
+
+    def end():
+        for _ in progress:
+            pass
+        for copy in z_copies:
+            copy.wait_send()
+
+    return progress, need, end
 
 
 def halving(order, n_dp, half, grads, out_buf, in_buf, send, recv, load_sem):
@@ -304,7 +291,8 @@
 
         yield from doubling(order, n_dp, half, buf, d_send, d_recv, ready)
 
-    staggered([lane(half) for half in range(halves)])
+    for _ in staggered([lane(half) for half in range(halves)]):
+        pass
     for copy in z_copies:
         copy.wait_send()
     exchange_finish(n_dp, started, got_events, ev_recv)
@@ -369,11 +357,14 @@
 
 
 def window_kernel(
-    sizes, slots, full, unit_table, session_table, target, grads, grad_tokens,
+    grid, sizes, ids, attn, read, latents, unit_table, session_table, target, grads, grad_tokens,
+    got_ids, full, id_send, id_recv, z_send, send, recv, local,
     tokens, normed, keys, values, query, mixed, gmixed, gquery, gkeys, gvalues, lat, lnorm, peak, scale,
     resid, ring, sems,
 ):
+    n_dp, n_f, halves, lane_rows, slot_count = grid
     n_f, own, read_rows, lat_rows, out_width = sizes
+    mine = lax.axis_index("fsdp")
     width = tokens.shape[1]
     low = jnp.bfloat16
     base_read = 4 * own
@@ -381,6 +372,30 @@
     end = base_lat + lat_rows
     times = width // out_width
     W_Q, W_K, W_V, W_O = range(4)
+    padded = full.shape[1]
+    place = (padded - 2 * own, 0, own, padded - own)
+    at_lat = 2 * own
+    at_read = at_lat + lat_rows
+    filled = at_read + read_rows
+
+    moves = [(attn.at[k], full.at[mine, pl.ds(place[k], own)]) for k in range(4)]
+    moves.append((latents, full.at[mine, pl.ds(at_lat, lat_rows)]))
+    for t in range(times):
+        moves.append((
+            read.at[pl.ds(t * read_rows, read_rows)],
+            full.at[mine, pl.ds(at_read, read_rows), pl.ds(t * out_width, out_width)],
+        ))
+    moves = [pltpu.make_async_copy(src, dst, local.at[1 + n]) for n, (src, dst) in enumerate(moves)]
+    for move in moves:
+        move.start()
+    if filled < place[W_Q]:
+        full[mine, filled:place[W_Q]] = jnp.zeros((place[W_Q] - filled, width), low)
+    greet(n_dp, n_f)
+    started = exchange_start(n_dp, ids, got_ids, id_send, id_recv, local.at[0])
+    for move in moves:
+        move.wait()
+    progress, need, end_gather = gather(n_dp, n_f, halves, lane_rows, full, z_send, send, recv)
+    exchange_finish(n_dp, started, got_ids, id_recv)
     state = {"n": 0, "busy": [None] * ring.shape[0]}
 
     def put(f, row, value):
@@ -400,7 +415,7 @@
         return slice(f * own, (f + 1) * own)
 
     def block(k, f):
-        return full[f, k * own:(k + 1) * own]
+        return full[f, place[k]:place[k] + own]
 
     def times_weight(left, k):
         total = dot_nn(left[:, cols(0)], block(k, 0))
@@ -412,7 +427,12 @@
         for f in range(n_f):
             put(f, k * own, dot_tn(left[:, cols(f)], right[...]))
 
-    slots_unit, slots_session, live = slots[0:1], slots[1:2], slots[2:3] > 0
+    def slots(k):
+        return jnp.concatenate(
+            [got_ids[d, :, k * slot_count:(k + 1) * slot_count] for d in range(n_dp)], axis=1
+        )
+
+    slots_unit, slots_session, live = slots(0), slots(1), slots(2) > 0
     events = tokens.shape[0]
 
     def pick(table, ids, start, count):
@@ -428,10 +448,13 @@
     tokens[...] = total.astype(low)
     rows = tokens[...].astype(jnp.float32)
     normed[...] = (rows * rms_scale(rows)).astype(low)
+    need(own)
     keys[...] = times_weight(normed, W_K).astype(low)
+    need(2 * own)
     values[...] = times_weight(normed, W_V).astype(low)
+    need(place[W_Q] + own)
     for f in range(n_f):
-        lat[f * lat_rows:(f + 1) * lat_rows] = full[f, base_lat:end]
+        lat[f * lat_rows:(f + 1) * lat_rows] = full[f, at_lat:at_lat + lat_rows]
     query[...] = times_weight(lat, W_Q).astype(low)
 
     latent_count = lat.shape[0]
@@ -471,6 +494,7 @@
 
     lax.fori_loop(0, width // 128, forward, 0)
 
+    end_gather()
     resid[...] = lat[...].astype(jnp.float32) + times_weight(mixed, W_O)
     factor = rms_scale(resid[...])
     lnorm[...] = (resid[...] * factor).astype(low)
@@ -480,7 +504,7 @@
         for f in range(n_f):
             for t in range(times):
                 at = f * own + t * step
-                yield f, t, slice(at, at + step), full[f, base_read:base_lat, t * out_width:(t + 1) * out_width]
+                yield f, t, slice(at, at + step), full[f, at_read:filled, t * out_width:(t + 1) * out_width]
 
     logits = None
     for f, t, at, weight in pieces():
@@ -546,25 +570,35 @@
             copy.wait()
 
 
-def window_grads(sizes, slots, full, unit_table, session_table, target):
+def window_grads(grid, sizes, ids, attn, read, latents, unit_table, session_table, target):
+    n_dp, n_f, halves, lane_rows, slot_count = grid
     n_f, own, read_rows, lat_rows, out_width = sizes
-    events, width = slots.shape[1], full.shape[-1]
+    events, width = n_dp * slot_count, attn.shape[-1]
     latent_count = n_f * lat_rows
     low = jnp.bfloat16
-    spare = full.shape[1] - 4 * own - read_rows - lat_rows
-    ring_rows = max(own, spare)
+    padded = halves * n_dp * lane_rows
+    ring_rows = max(own, padded - 4 * own - read_rows - lat_rows)
     by_event = pltpu.VMEM((events, width), low)
     by_latent = pltpu.VMEM((latent_count, width), low)
     column = pltpu.VMEM((HEADS, latent_count, 1), jnp.float32)
+    in_vmem, anywhere = pl.BlockSpec(memory_space=pltpu.VMEM), pl.BlockSpec(memory_space=pl.ANY)
     return pl.pallas_call(
-        functools.partial(window_kernel, sizes),
+        functools.partial(window_kernel, grid, sizes),
         out_shape=(
-            jax.ShapeDtypeStruct(full.shape, jnp.float32),
+            jax.ShapeDtypeStruct((n_f, padded, width), jnp.float32),
             jax.ShapeDtypeStruct((events, width), low),
         ),
-        in_specs=[pl.BlockSpec(memory_space=pltpu.VMEM)] * 5,
-        out_specs=[pl.BlockSpec(memory_space=pl.ANY), pl.BlockSpec(memory_space=pltpu.VMEM)],
+        in_specs=[in_vmem] + [anywhere] * 3 + [in_vmem] * 3,
+        out_specs=[anywhere, in_vmem],
         scratch_shapes=[
+            pltpu.VMEM(ids.shape, ids.dtype),
+            pltpu.VMEM((n_f, padded, width), low),
+            pltpu.SemaphoreType.DMA((n_dp,)),
+            pltpu.SemaphoreType.DMA((n_dp,)),
+            pltpu.SemaphoreType.DMA((halves, n_f)),
+            pltpu.SemaphoreType.DMA((n_f, halves, n_dp)),
+            pltpu.SemaphoreType.DMA((n_f, halves, n_dp)),
+            pltpu.SemaphoreType.DMA((6 + width // out_width,)),
             by_event, by_event, by_event, by_event,
             by_latent, by_latent, by_latent, by_latent,
             by_event, by_event, by_latent, by_latent, column, column,
@@ -572,8 +606,10 @@
             pltpu.VMEM((4, ring_rows, width), jnp.float32),
             pltpu.SemaphoreType.DMA((4,)),
         ],
-        compiler_params=pltpu.CompilerParams(vmem_limit_bytes=60 * MIB),
-    )(slots, full, unit_table, session_table, target)
+        compiler_params=pltpu.CompilerParams(
+            collective_id=0, has_side_effects=True, vmem_limit_bytes=60 * MIB
+        ),
+    )(ids, attn, read, latents, unit_table, session_table, target)
 
 
 def piece_rows(rows, n_dp):
@@ -583,14 +619,6 @@
         options.append((lane_rows * lanes, -lanes, lane_rows))
     _, lanes, lane_rows = min(options)
     return lane_rows, -lanes
-
-
-def fold(rows, width):
-    times = width // rows.shape[-1]
-    step = rows.shape[-2] // times
-    return jnp.concatenate(
-        [rows[..., k * step:(k + 1) * step, :] for k in range(times)], axis=-1
-    )
 
 
 def unfold(rows, narrow):
@@ -632,22 +660,13 @@
         axis=1,
     )
     id_rows = jnp.pad(id_rows, ((0, 0), (0, 128 - id_rows.shape[1]))).reshape(n_dp, 1, 128)
-    shard = jnp.concatenate(
-        [
-            attn_weights.reshape(stack * own_rows, width),
-            fold(read_weight, width),
-            latents,
-            jnp.zeros((padded - ends[2], width), jnp.bfloat16),
-        ]
-    ).reshape(n_dp, halves, rows, width)
-    got_ids, full = gather_params(n_dp, n_f, id_rows, shard)
-    full = full.reshape(n_f, padded, width)
-    sizes = (n_f, own_rows, read_rows, lat_rows, out_width)
-    slots = jnp.transpose(got_ids[:, 0, :3 * slot_count].reshape(n_dp, 3, slot_count), (1, 0, 2))
     grads, grad_tokens = window_grads(
-        sizes,
-        slots.reshape(3, event_total),
-        full,
+        (n_dp, n_f, halves, rows, slot_count),
+        (n_f, own_rows, read_rows, lat_rows, out_width),
+        id_rows,
+        attn_weights,
+        read_weight,
+        latents,
         unit_table,
         session_table,
         targets.reshape(targets.shape[-2], out_width),

time: 212 us -> 191 us (0.901)
  Pallas kernels: 188 us -> 180 us
  other arithmetic: 13.6 us -> 6.47 us
  local copies, waits for them, and re-layouts: 9.34 us -> 4.14 us
    concatenate x1 -> x0, other arithmetic: 7.1 us -> none  [on_device(): jnp.concatenate([attn_weights.reshape(stack * own_rows, width), fold(read...]
    pallas_call x2 -> x1, Pallas kernels: 95.8 us -> 89.7 us  [window_grads(): pl.pallas_call(functools.partial(window_kernel, grid, sizes), out_shape=(...]
    unnamed x5 -> x3, local copies, waits for them, and re-layouts: 4.75 us -> 0.8 us
    pallas_call x1, Pallas kernels: 92.6 us -> 90.2 us  [reduce_grads(): pl.pallas_call(functools.partial(reduce_kernel, n_dp, n_f, halves), out_s...]
where the time goes in v2:
time: 191 us
  Pallas kernels  180 us (94%)
  other arithmetic  6.47 us (3%)
  local copies, waits for them, and re-layouts  4.14 us (2%)
    pallas_call x1, Pallas kernels, reduce_grads(): pl.pallas_call(functools.partial(reduce_kernel, n_dp, n_f, halves), out_s...  90.2 us
    pallas_call x1, Pallas kernels, window_grads(): pl.pallas_call(functools.partial(window_kernel, grid, sizes), out_shape=(...  89.7 us

profile of v2, /device:TPU:0, one launch (start us, length us, event | category | flops | bytes accessed | tf_op | source)
XLA Modules:
  0.0 191.1 jit_solution(16289106153814526629)
XLA Ops:
  0.6 0.7 fusion
  1.4 0.8 pad_add_fusion
  2.1 0.6 pad.4
  2.7 89.7 %shard_map.120 = (f32[4,1280,1024]{2,1,0:T(8,128)}, bf16[256,1024]{1,0:T(8,128)(2,1)}) custom-call(s32[8,1,128]{2,1,0:T(1,128)} %bitcast.19, bf16[4,256,1024]{2,1,0:T(8,128)(2,1)} %attn.1, bf16[256,512]{1,0:T(8,128)(2,1)} %read.1, bf16[64,1024]{1,0:T(8,128)(2,1)} %latents.1, bf16[2048,1024]{1,0:T(8,128)(2,1)} %unit_table.1, bf16[64,1024]{1,0:T(8,128)(2,1)} %session_table.1, ...), custom_call_target="tpu_custom_call" | custom-call | tf_op jit(solution)/shard_map/pallas_call | solution.py:585
  92.4 90.2 %shard_map.121 = (bf16[8,5,32,1024]{3,2,1,0:T(8,128)(2,1)}, bf16[8,32,1024]{2,1,0:T(8,128)(2,1)}) custom-call(f32[4,8,5,32,1024]{4,3,2,1,0:T(8,128)} %bitcast.11, bf16[8,32,1024]{2,1,0:T(8,128)(2,1)} %bitcast.18), custom_call_target="tpu_custom_call" | custom-call | tf_op jit(solution)/shard_map/pallas_call | solution.py:304
  182.6 1.6 slice_convert_fusion
  184.2 1.0 fusion.1
  185.2 1.8 slice.19
  187.0 0.9 maximum_convert_fusion
  187.9 0.0 copy-start
  187.9 2.5 %convert.1 = f32[4,256,1024]{2,1,0:T(8,128)} convert(bf16[4,256,1024]{2,1,0:T(8,128)(2,1)S(1)} %bitcast.12) | non-fusion elementwise | flops 1048576 | bytes 6291456 | tf_op jit(solution)/shard_map/convert_element_type | solution.py:681
  190.3 0.0 copy-done
  190.3 0.8 copy.14
Async XLA Ops:
  187.9 2.5 %copy-start = (bf16[8,32,1024]{2,1,0:T(8,128)(2,1)S(1)}, bf16[8,32,1024]{2,1,0:T(8,128)(2,1)}, u32[]{:S(2)}) copy-start(bf16[8,32,1024]{2,1,0:T(8,128)(2,1)} %get-tuple-element.10) | copy-start | bytes 1572868

commit v3 on v2

--- a/solution.py
+++ b/solution.py
@@ -116,8 +116,7 @@
 def staggered(walks):
     waiting, active = list(walks), []
     while waiting or active:
-        if waiting:
-            active.append(waiting.pop(0))
+        active, waiting = active + waiting[:2], waiting[2:]
         still = []
         for walk in active:
             if next(walk, None) is not None:

time: 191 us -> 177 us (0.927)
  Pallas kernels: 180 us -> 165 us
    pallas_call x1, Pallas kernels: 90.2 us -> 77.6 us  [reduce_grads(): pl.pallas_call(functools.partial(reduce_kernel, n_dp, n_f, halves), out_s...]
where the time goes in v3:
time: 177 us
  Pallas kernels  165 us (93%)
  other arithmetic  6.47 us (4%)
  local copies, waits for them, and re-layouts  4.14 us (2%)
    pallas_call x1, Pallas kernels, window_grads(): pl.pallas_call(functools.partial(window_kernel, grid, sizes), out_shape=(...  87.9 us
    pallas_call x1, Pallas kernels, reduce_grads(): pl.pallas_call(functools.partial(reduce_kernel, n_dp, n_f, halves), out_s...  77.6 us

profile of v3, /device:TPU:0, one launch (start us, length us, event | category | flops | bytes accessed | tf_op | source)
XLA Modules:
  0.0 176.7 jit_solution(15927662127521268776)
XLA Ops:
  0.6 0.7 fusion
  1.4 0.8 pad_add_fusion
  2.1 0.6 pad.4
  2.7 87.9 %shard_map.120 = (f32[4,1280,1024]{2,1,0:T(8,128)}, bf16[256,1024]{1,0:T(8,128)(2,1)}) custom-call(s32[8,1,128]{2,1,0:T(1,128)} %bitcast.19, bf16[4,256,1024]{2,1,0:T(8,128)(2,1)} %attn.1, bf16[256,512]{1,0:T(8,128)(2,1)} %read.1, bf16[64,1024]{1,0:T(8,128)(2,1)} %latents.1, bf16[2048,1024]{1,0:T(8,128)(2,1)} %unit_table.1, bf16[64,1024]{1,0:T(8,128)(2,1)} %session_table.1, ...), custom_call_target="tpu_custom_call" | custom-call | tf_op jit(solution)/shard_map/pallas_call | solution.py:584
  90.6 77.6 %shard_map.121 = (bf16[8,5,32,1024]{3,2,1,0:T(8,128)(2,1)}, bf16[8,32,1024]{2,1,0:T(8,128)(2,1)}) custom-call(f32[4,8,5,32,1024]{4,3,2,1,0:T(8,128)} %bitcast.11, bf16[8,32,1024]{2,1,0:T(8,128)(2,1)} %bitcast.18), custom_call_target="tpu_custom_call" | custom-call | tf_op jit(solution)/shard_map/pallas_call | solution.py:303
  168.2 1.6 slice_convert_fusion
  169.8 1.0 fusion.1
  170.8 1.8 slice.19
  172.6 0.9 maximum_convert_fusion
  173.5 0.0 copy-start
  173.5 2.5 %convert.1 = f32[4,256,1024]{2,1,0:T(8,128)} convert(bf16[4,256,1024]{2,1,0:T(8,128)(2,1)S(1)} %bitcast.12) | non-fusion elementwise | flops 1048576 | bytes 6291456 | tf_op jit(solution)/shard_map/convert_element_type | solution.py:680
  175.9 0.0 copy-done
  175.9 0.8 copy.14
Async XLA Ops:
  173.5 2.5 %copy-start = (bf16[8,32,1024]{2,1,0:T(8,128)(2,1)S(1)}, bf16[8,32,1024]{2,1,0:T(8,128)(2,1)}, u32[]{:S(2)}) copy-start(bf16[8,32,1024]{2,1,0:T(8,128)(2,1)} %get-tuple-element.10) | copy-start | bytes 1572868
